TPU v7x, 32 devices: a whole 2x2x4 slice. The times are simulated.
32 devices in a mesh: batch: 4 (over y, x), seq: 8 (over z, core).
Axes of the slice: x: 2, y: 2, z: 4, core: 2. Of those that a mesh axis runs over, the one named last changes fastest.
Arguments:
- inputs: bfloat16 [4, 8192, 312], P('batch', 'seq'), may hold values from -6 to 6
- teacher_input: bfloat16 [4, 8192, 768], P('batch', 'seq'), may hold values from -6 to 6
- filled_slot_mask: int32 [4, 8192], P('batch'), may hold values 0 or 1
- seg_lengths: int32 [4, 32], P('batch'), may hold values from 1 to 511, as said below
- query_weight: bfloat16 [312, 312], replicated, may hold values from -0.3125 to 0.3125
- key_weight: bfloat16 [312, 312], replicated, may hold values from -0.3125 to 0.3125
- value_weight: bfloat16 [312, 312], replicated, may hold values from -0.3125 to 0.3125
- w_output: bfloat16 [312, 312], replicated, may hold values from -3.5 to 3.5
- gain_one: float32 [312], replicated, may hold values from 0.1 to 1.9
- shift_one: float32 [312], replicated, may hold values from -1.8 to 1.8
- w_inner: bfloat16 [312, 1200], replicated, may hold values from -0.3125 to 0.3125
- b_inner: float32 [1200], replicated, may hold values from -3 to 3
- w_outer: bfloat16 [1200, 312], replicated, may hold values from -0.1875 to 0.1875
- b_outer: float32 [312], replicated, may hold values from -1.8 to 1.8
- gain_two: float32 [312], replicated, may hold values from 0.1 to 1.9
- shift_two: float32 [312], replicated, may hold values from -1.8 to 1.8
- w_hidden: bfloat16 [312, 768], replicated, may hold values from -0.3125 to 0.3125
- teacher_query_weight: bfloat16 [768, 768], replicated, may hold values from -0.21875 to 0.21875
- teacher_key_weight: bfloat16 [768, 768], replicated, may hold values from -0.21875 to 0.21875
- teacher_value_weight: bfloat16 [768, 768], replicated, may hold values from -0.21875 to 0.21875
- teacher_output: bfloat16 [768, 768], replicated, may hold values from -2 to 2
- teacher_gain_one: float32 [768], replicated, may hold values from 0.1 to 1.9
- teacher_shift_one: float32 [768], replicated, may hold values from -1.8 to 1.8
- teacher_inner: bfloat16 [768, 3072], replicated, may hold values from -0.21875 to 0.21875
- teacher_outer: bfloat16 [3072, 768], replicated, may hold values from -0.109375 to 0.109375
- teacher_gain_two: float32 [768], replicated, may hold values from 0.1 to 1.9
- teacher_shift_two: float32 [768], replicated, may hold values from -1.8 to 1.8
Outputs:
- student_out: bfloat16 [4, 8192, 312], P('batch', 'seq')
- grad_inputs: bfloat16 [4, 8192, 312], P('batch', 'seq')
- loss: float32 [], replicated
- grad_w_query: float32 [312, 312], replicated
- grad_w_key: float32 [312, 312], replicated
- grad_w_value: float32 [312, 312], replicated
- grad_w_output: float32 [312, 312], replicated
- grad_gain_one: float32 [312], replicated
- grad_shift_one: float32 [312], replicated
- grad_w_inner: float32 [312, 1200], replicated
- grad_b_inner: float32 [1200], replicated
- grad_w_outer: float32 [1200, 312], replicated
- grad_b_outer: float32 [312], replicated
- grad_gain_two: float32 [312], replicated
- grad_shift_two: float32 [312], replicated
- grad_w_hidden: float32 [312, 768], replicated
Inputs may be any that keep to these rules, and one draw needn't show every extreme that they name: `seg_lengths`: the segments of a row tile its 8192 slots in order from the first. Exactly one segment starts in each aligned window of 256 slots, and no segment starts at the first slot of a device's 1024 slots except the row's first.
All inputs are finite; a program needn't handle non-finite values. No bound on the sum of `filled_slot_mask` on one device may be relied on, other than what follows from the above.
Results may differ from a plain program's by a relative error of at most 0.0095.
Values may be sent and summed in bfloat16 or wider, within the bound.
A program may use at most 384 MiB of HBM per device.

v0:
```python
from functools import partial

import jax
import jax.numpy as jnp
from jax import lax
from jax.experimental import pallas as pl
from jax.experimental.pallas import tpu as pltpu
from jax.sharding import PartitionSpec as P

HEADS = 12
HD_S = 26
HD_T = 64
WIN = 256
PAD = 32
SLOT_ONE = 26
PAIRS = HEADS // 2
CHUNK = 64
TAIL = 16
SLOTS = 4
BLOCK = 320
STRIP = 64
STRIP_OUTER = 384
STRIP_BIAS = 768
QKV_LANES = 384
MESH = pl.DeviceIdType.MESH
EPSILON = 1e-05
NEGATIVE = -1e30
LOG2E = 1.4426950408889634
F32 = jnp.float32
BF16 = jnp.bfloat16
VMEM = pl.BlockSpec(memory_space=pltpu.VMEM)
BIG = 60 << 20


def mm(left, right, dims):
    return lax.dot_general(left, right, ((dims[:1], dims[1:]), ((), ())), preferred_element_type=F32)


def nn(left, right):
    return mm(left, right, (1, 0))


def tn(left, right):
    return mm(left, right, (0, 0))


def nt(left, right):
    return mm(left, right, (1, 1))


def tt(left, right):
    return mm(left, right, (0, 1))


def pad_heads():
    row = lax.broadcasted_iota(jnp.int32, (HEADS * PAD, HEADS * HD_S), 0)
    col = lax.broadcasted_iota(jnp.int32, (HEADS * PAD, HEADS * HD_S), 1)
    spot = jnp.zeros((HEADS * PAD, HEADS * HD_S), F32)
    for head in range(HEADS):
        here = (row - head * PAD == col - head * HD_S) & (col >= head * HD_S) & (col < (head + 1) * HD_S)
        spot = jnp.where(here, 1.0, spot)
    return spot.astype(BF16)


def window_rows(mask_ref, lengths_ref, seq_index, windows, row_windows):
    lengths = lengths_ref[...].astype(F32)
    order = lax.broadcasted_iota(jnp.int32, lengths.shape, 1)
    lane = lax.broadcasted_iota(jnp.int32, (1, WIN), 1).astype(F32)
    out = []
    for j in range(windows + 2):
        number = seq_index * windows + (j - 1)
        inside = (number >= 0) & (number < row_windows)
        safe = jnp.clip(number, 0, row_windows - 1)
        start = jnp.sum(jnp.where(order < safe, lengths, 0.0), axis=1, keepdims=True)
        offset = start - (safe * WIN).astype(F32)
        late = (lane >= offset).astype(F32)
        filled = mask_ref[:, pl.ds(pl.multiple_of(safe * WIN, WIN), WIN)]
        filled = jnp.where(inside, filled.astype(F32), 0.0)
        out.append((late, filled))
    return out


def stack_rows(*rows):
    n = rows[0].shape[1]
    index = lax.broadcasted_iota(jnp.int32, (8, n), 0)
    block = jnp.zeros((8, n), F32)
    for k, row in enumerate(rows):
        block = jnp.where(index == k, row, block)
    return block.astype(BF16)


def attend_kernel(
    windows,
    row_windows,
    mask_ref,
    lengths_ref,
    xt_hbm,
    xs_ref,
    wtq_hbm,
    wtk_hbm,
    wtv_hbm,
    wq_ref,
    wk_ref,
    wv_ref,
    stats_ref,
    loss_ref,
    rows_ref,
    tctx_hbm,
    sctx_hbm,
    sq_hbm,
    skv_hbm,
    saved_e_hbm,
    saved_g_hbm,
    x_ref,
    xs_side_ref,
    wt_ref,
    bias_ref,
    wst_ref,
    tq_ref,
    tk_ref,
    tv_ref,
    sq_ref,
    skv_ref,
    tctx_ref,
    sctx_ref,
    e_ref,
    g_ref,
    work_ref,
    low_ref,
    in_sem,
    halo_send,
    halo_arrive,
    kv_sem,
    out_sem,
):
    slots = windows * WIN
    batch, seq = lax.axis_index("batch"), lax.axis_index("seq")
    peers = lax.axis_size("seq")
    has_left, has_right = seq > 0, seq < peers - 1
    width_t = x_ref.shape[1]
    extended = slots + 2 * WIN

    barrier = pltpu.get_barrier_semaphore()
    for move in (1, peers - 1):
        pl.semaphore_signal(barrier, inc=1, device_id=(batch, (seq + move) % peers), device_id_type=MESH)
    loads = [pltpu.make_async_copy(xt_hbm, x_ref.at[pl.ds(WIN, slots)], in_sem.at[0])]
    for k, w_hbm in enumerate((wtq_hbm, wtk_hbm, wtv_hbm)):
        loads.append(pltpu.make_async_copy(w_hbm, wt_ref.at[k], in_sem.at[1 + k]))
    for c in loads:
        c.start()
    pl.semaphore_wait(barrier, 2)

    def halo(side):
        device = (batch, seq - 1 + 2 * side)
        first = pl.multiple_of(side * (slots - WIN), WIN)
        return [
            pltpu.make_async_remote_copy(
                src_ref=xt_hbm.at[pl.ds(first, WIN)],
                dst_ref=x_ref.at[pl.ds(pl.multiple_of((1 - side) * (WIN + slots), WIN), WIN)],
                send_sem=halo_send.at[0, side],
                recv_sem=halo_arrive.at[0, 1 - side],
                device_id=device,
                device_id_type=MESH,
            ),
            pltpu.make_async_remote_copy(
                src_ref=xs_ref.at[:, pl.ds(first, WIN)],
                dst_ref=xs_side_ref.at[1 - side],
                send_sem=halo_send.at[1, side],
                recv_sem=halo_arrive.at[1, 1 - side],
                device_id=device,
                device_id_type=MESH,
            ),
        ]

    for side, present in ((0, has_left), (1, has_right)):

        @pl.when(present)
        def _():
            for c in halo(side):
                c.start()

        @pl.when(jnp.logical_not(present))
        def _():
            x_ref[side * (WIN + slots) : side * (WIN + slots) + WIN, :] = jnp.zeros((WIN, width_t), BF16)
            xs_side_ref[side] = jnp.zeros(xs_side_ref.shape[1:], BF16)

    info = window_rows(mask_ref, lengths_ref, seq, windows, row_windows)
    eye = lax.broadcasted_iota(jnp.int32, (WIN, WIN), 0) == lax.broadcasted_iota(jnp.int32, (WIN, WIN), 1)
    rows_ref[...] = jnp.zeros_like(rows_ref)
    for w in range(windows):
        late, filled = info[w + 1]
        late_l, filled_l = info[w]
        late_r, filled_r = info[w + 2]
        early = 1.0 - late
        here = slice(w * WIN, (w + 1) * WIN)
        rows_ref[0:1, here] = early
        rows_ref[1:2, here] = late
        rows_ref[2:3, here] = filled
        query = stack_rows(early, late)
        own = tn(stack_rows(NEGATIVE * (1.0 - early * filled), NEGATIVE * (1.0 - late * filled)), query)
        bias_ref[w, :WIN, :] = jnp.where(eye, 0.0, own)
        bias_ref[w, WIN:, :] = tn(
            stack_rows(
                NEGATIVE * (1.0 - late_l * filled_l), NEGATIVE * (1.0 - (1.0 - late_r) * filled_r)
            ),
            query,
        )
    loss_ref[...] = jnp.zeros_like(loss_ref)
    stats_ref[...] = jnp.zeros_like(stats_ref)
    spot = pad_heads()
    padded = HEADS * PAD
    row = lax.broadcasted_iota(jnp.int32, (padded, 1), 0) % PAD
    ones = (row >= SLOT_ONE) & (row < SLOT_ONE + 3)

    xs = xs_ref[...]
    for k, w_ref in enumerate((wq_ref, wk_ref, wv_ref)):
        wst_ref[k] = nt(spot, w_ref[...]).astype(BF16)
        made = nn(wst_ref[k], xs)
        if k == 0:
            sq_ref[...] = (made * (LOG2E * HD_S**-0.5)).astype(BF16)
        else:
            if k == 2:
                made = jnp.where(ones, 1.0, made)
            skv_ref[k - 1, :, WIN : WIN + slots] = made.astype(BF16)
    tail = (lax.broadcasted_iota(jnp.int32, (TAIL, extended), 0) == 0).astype(BF16)
    for head in range(HEADS):
        tv_ref[head * (HD_T + TAIL) + HD_T : (head + 1) * (HD_T + TAIL), :] = tail

    def put_values(made, first_head, lanes):
        for j in range(made.shape[0] // HD_T):
            at = pl.multiple_of((first_head + j) * (HD_T + TAIL), TAIL)
            tv_ref[pl.ds(at, HD_T), lanes] = made[j * HD_T : (j + 1) * HD_T]

    part = width_t // 2
    loads[0].wait()
    for k in range(3):
        loads[1 + k].wait()

        def project(half, carry, k=k):
            rows = pl.ds(pl.multiple_of(half * part, 128), part)
            made = tt(wt_ref[k, :, rows], x_ref[WIN : WIN + slots, :])
            if k == 0:
                tq_ref[rows, :] = (made * (LOG2E * HD_T**-0.5)).astype(BF16)
            elif k == 1:
                tk_ref[rows, WIN : WIN + slots] = made.astype(BF16)
            else:
                put_values(made.astype(BF16), half * (HEADS // 2), slice(WIN, WIN + slots))
            return carry

        lax.fori_loop(0, 2, project, 0)

    def project_side(side, carry):
        @pl.when(jnp.where(side == 0, has_left, has_right))
        def _():
            for sent, landed in zip(halo(side), halo(1 - side)):
                sent.wait_send()
                landed.wait_recv()

        lanes = pl.ds(pl.multiple_of(side * (WIN + slots), WIN), WIN)
        for k in (1, 2):
            made = tt(wt_ref[k], x_ref[lanes, :]).astype(BF16)
            if k == 1:
                tk_ref[:, lanes] = made
            else:
                put_values(made, 0, lanes)
            made = nn(wst_ref[k], xs_side_ref[side])
            if k == 2:
                made = jnp.where(ones, 1.0, made)
            skv_ref[k - 1, :, lanes] = made.astype(BF16)
        return carry

    lax.fori_loop(0, 2, project_side, 0)
    finals = [
        pltpu.make_async_copy(sq_ref, sq_hbm, kv_sem.at[0]),
        pltpu.make_async_copy(skv_ref, skv_hbm, kv_sem.at[1]),
    ]
    for c in finals:
        c.start()

    def stores(pair, which):
        slot = pair % 2
        t_rows = pl.ds(pl.multiple_of(pair * 2 * HD_T, 2 * HD_T), 2 * HD_T)
        s_rows = pl.ds(pl.multiple_of(pair * 2 * PAD, 2 * PAD), 2 * PAD)
        heads = pl.ds(pair * 2, 2)
        ends = (
            (e_ref.at[slot], saved_e_hbm.at[:, heads]),
            (g_ref.at[slot], saved_g_hbm.at[:, heads]),
            (tctx_ref.at[t_rows], tctx_hbm.at[t_rows]),
            (sctx_ref.at[s_rows], sctx_hbm.at[s_rows]),
        )
        return [pltpu.make_async_copy(*ends[k], out_sem.at[k, pair]) for k in which]

    def one_pair(pair, carry):
        @pl.when(pair >= 2)
        def _():
            for c in stores(pair - 2, (0, 1)):
                c.wait()

        attend_pair(pair)
        for c in stores(pair, range(4)):
            c.start()
        return carry

    def attend_pair(pair):
        e_out, g_out = e_ref.at[pair % 2], g_ref.at[pair % 2]
        def rows_of(w):
            left = slice(w * WIN, (w + 1) * WIN)
            own = slice((w + 1) * WIN, (w + 2) * WIN)
            right = slice((w + 2) * WIN, (w + 3) * WIN)
            return left, own, right, rows_ref[0:1, left], rows_ref[1:2, left], rows_ref[2:3, left]

        def first_pass(w, q_ref, k_ref, rows, work_ref):
            left, own, right, early, late, _ = rows_of(w)
            query = q_ref[rows, left]
            query_fold = jnp.concatenate([query * early.astype(BF16), query * late.astype(BF16)], axis=0)
            keys = k_ref[rows, own]
            keys_fold = jnp.concatenate([k_ref[rows, left], k_ref[rows, right]], axis=0)
            top = None
            for part, (a, b) in enumerate(((keys, query), (keys_fold, query_fold))):
                raw = tn(a, b)
                for c in range(0, WIN, CHUNK):
                    block = raw[c : c + CHUNK] + bias_ref[w, part * WIN + c : part * WIN + c + CHUNK, :]
                    work_ref[part * WIN + c : part * WIN + c + CHUNK, :] = block
                    for r in range(0, CHUNK, 8):
                        piece = block[r : r + 8]
                        top = piece if top is None else jnp.maximum(top, piece)
            return jnp.max(top, axis=0, keepdims=True)

        def second_pass(work_ref, top, low_ref):
            for c in range(0, 2 * WIN, CHUNK):
                e = jnp.exp2(work_ref[c : c + CHUNK, :] - top)
                work_ref[c : c + CHUNK, :] = e
                low_ref[c : c + CHUNK, :] = e.astype(BF16)

        def mix(w, v_ref, rows, low_ref, head_width):
            left, own, right, early, late, _ = rows_of(w)
            values = v_ref[rows, own]
            values_fold = jnp.concatenate([v_ref[rows, left], v_ref[rows, right]], axis=0)
            mixed = nn(values, low_ref[:WIN, :])
            side = nn(values_fold, low_ref[WIN:, :])
            n = values.shape[0]
            mixed = mixed + early * side[:n] + late * side[n:]
            inverse = 1.0 / mixed[head_width : head_width + 1]
            return mixed[: -TAIL if head_width == HD_T else n] * inverse, inverse

        units = [(w, h) for w in range(windows) for h in range(2)]
        state = {}

        def refs(u):
            w, h = units[u]
            head = 2 * pair + h
            t_rows = pl.ds(pl.multiple_of(head * HD_T, HD_T), HD_T)
            s_rows = pl.ds(pl.multiple_of(head * PAD, PAD), PAD)
            v_rows = pl.ds(pl.multiple_of(head * (HD_T + TAIL), TAIL), HD_T + TAIL)
            slot = u % SLOTS
            return w, h, t_rows, s_rows, v_rows, work_ref.at[2 * slot], work_ref.at[2 * slot + 1], low_ref.at[slot]

        def score_stage(u):
            w, h, t_rows, s_rows, _, work_t, work_s, _ = refs(u)
            state[u] = [
                first_pass(w, tq_ref, tk_ref, t_rows, work_t),
                first_pass(w, sq_ref, skv_ref.at[0], s_rows, work_s),
            ]

        def power_stage(u):
            w, h, _, _, _, work_t, work_s, low_t = refs(u)
            second_pass(work_t, state[u][0], low_t)
            second_pass(work_s, state[u][1], e_out.at[w, h])

        def mix_stage(u):
            w, h, t_rows, s_rows, v_rows, _, _, low_t = refs(u)
            left = rows_of(w)[0]
            t_mixed, t_inv = mix(w, tv_ref, v_rows, low_t, HD_T)
            s_mixed, s_inv = mix(w, skv_ref.at[1], s_rows, e_out.at[w, h], SLOT_ONE)
            tctx_ref[t_rows, left] = t_mixed.astype(BF16)
            sctx_ref[s_rows, left] = s_mixed
            state[u] = [t_inv, s_inv]

        def gap_stage(u):
            w, h, _, _, _, work_t, work_s, _ = refs(u)
            left, _, _, _, _, filled = rows_of(w)
            t_inv, s_inv = state.pop(u)
            width = 2.0 * HEADS * HD_T
            scale_s = (width * filled) * s_inv * s_inv
            scale_t = (width * filled) * s_inv * t_inv
            square = jnp.zeros((8, WIN), F32)
            cross = jnp.zeros((8, WIN), F32)
            for c in range(0, 2 * WIN, CHUNK):
                s = work_s[c : c + CHUNK, :]
                gap = s * scale_s - work_t[c : c + CHUNK, :] * scale_t
                g_out[w, h, c : c + CHUNK, :] = gap.astype(BF16)
                for r in range(0, CHUNK, 8):
                    piece = gap[r : r + 8]
                    square += piece * piece
                    cross += piece * s[r : r + 8]
            square = jnp.sum(square, axis=0, keepdims=True)
            cross = jnp.sum(cross, axis=0, keepdims=True)
            back = 1.0 / (s_inv * width)
            stats_ref[pair, h : h + 1, left] = s_inv
            stats_ref[pair, 2 + h : 3 + h, left] = cross
            loss_ref[0:1, left] += square * back * back

        last = len(units)
        for u in range(last + 2):
            if u < last:
                score_stage(u)
            if 0 <= u - 1 < last:
                power_stage(u - 1)
            if 0 <= u - 2 < last:
                mix_stage(u - 2)
                gap_stage(u - 2)


    lax.fori_loop(0, PAIRS, one_pair, 0)
    for pair in range(PAIRS):
        for c in stores(pair, range(0 if pair >= PAIRS - 2 else 2, 4)):
            c.wait()
    for c in finals:
        c.wait()


def attend(mask, lengths, xt, xs, wtq, wtk, wtv, wq, wk, wv):
    slots, width_t = xt.shape
    width_s = xs.shape[0]
    windows = slots // WIN
    row_windows = mask.shape[1] // WIN
    padded = HEADS * PAD
    extended = slots + 2 * WIN
    sds = jax.ShapeDtypeStruct
    anywhere = pl.BlockSpec(memory_space=pl.ANY)
    saved = (windows, HEADS, 2 * WIN, WIN)
    return pl.pallas_call(
        partial(attend_kernel, windows, row_windows),
        out_shape=(
            sds((PAIRS, 8, slots), F32),
            sds((8, slots), F32),
            sds((8, slots), F32),
            sds((width_t, slots), BF16),
            sds((padded, slots), F32),
            sds((padded, slots), BF16),
            sds((2, padded, extended), BF16),
            sds(saved, BF16),
            sds(saved, BF16),
        ),
        in_specs=[VMEM, VMEM, anywhere, VMEM] + [anywhere] * 3 + [VMEM] * 3,
        out_specs=[VMEM] * 3 + [anywhere] * 6,
        scratch_shapes=[
            pltpu.VMEM((extended, width_t), BF16),
            pltpu.VMEM((2, width_s, WIN), BF16),
            pltpu.VMEM((3, width_t, width_t), BF16),
            pltpu.VMEM((windows, 2 * WIN, WIN), F32),
            pltpu.VMEM((3, padded, width_s), BF16),
            pltpu.VMEM((width_t, slots), BF16),
            pltpu.VMEM((width_t, extended), BF16),
            pltpu.VMEM((HEADS * (HD_T + TAIL), extended), BF16),
            pltpu.VMEM((padded, slots), BF16),
            pltpu.VMEM((2, padded, extended), BF16),
            pltpu.VMEM((width_t, slots), BF16),
            pltpu.VMEM((padded, slots), F32),
            pltpu.VMEM((2, windows, 2, 2 * WIN, WIN), BF16),
            pltpu.VMEM((2, windows, 2, 2 * WIN, WIN), BF16),
            pltpu.VMEM((2 * SLOTS, 2 * WIN, WIN), F32),
            pltpu.VMEM((SLOTS, 2 * WIN, WIN), BF16),
            pltpu.SemaphoreType.DMA((4,)),
            pltpu.SemaphoreType.DMA((2, 2)),
            pltpu.SemaphoreType.DMA((2, 2)),
            pltpu.SemaphoreType.DMA((2,)),
            pltpu.SemaphoreType.DMA((4, PAIRS)),
        ],
        compiler_params=pltpu.CompilerParams(
            vmem_limit_bytes=BIG, collective_id=1, has_side_effects=True
        ),
    )(mask, lengths, xt, xs, wtq, wtk, wtv, wq, wk, wv)


def normalize(values, gain, shift):
    n = values.shape[0]
    center = values - jnp.sum(values, axis=0, keepdims=True) * (1.0 / n)
    rscale = lax.rsqrt(jnp.sum(center * center, axis=0, keepdims=True) * (1.0 / n) + EPSILON)
    unit = center * rscale
    return unit * gain + shift, unit, rscale


def normalize_back(grad, unit, rscale, gain):
    n = grad.shape[0]
    scaled = grad * gain
    first = jnp.sum(scaled, axis=0, keepdims=True) * (1.0 / n)
    second = jnp.sum(scaled * unit, axis=0, keepdims=True) * (1.0 / n)
    return rscale * (scaled - first - unit * second)


def fold_lanes(values):
    total = values[:, :128]
    for at in range(128, values.shape[1], 128):
        total = total + values[:, at : at + 128]
    return total


ROOT_HALF = 0.7071067811865476
ROOT_PI = 0.3989422804014327


DENSE_IN = ("xt", "tctx", "two", "xs", "sctx", "tin", "tout", "wo", "w1", "w2", "wh")


def dense_kernel(
    xt_hbm,
    tctx_hbm,
    two_hbm,
    xs_hbm,
    sctx_hbm,
    tin_hbm,
    tout_hbm,
    wo_hbm,
    w1_hbm,
    w2_hbm,
    wh_hbm,
    stats_ref,
    rows_ref,
    loss_ref,
    t_gain_one_ref,
    t_shift_one_ref,
    t_gain_two_ref,
    t_shift_two_ref,
    gain_one_ref,
    shift_one_ref,
    b_outer_ref,
    gain_two_ref,
    shift_two_ref,
    b_inner_ref,
    out_hbm,
    dctx_hbm,
    dres_hbm,
    pack_hbm,
    xt_ref,
    tctx_ref,
    two_ref,
    xs_ref,
    sctx_ref,
    tin_ref,
    tout_ref,
    wo_ref,
    w1_ref,
    w2_ref,
    wh_ref,
    out_ref,
    dctx_ref,
    dres_ref,
    pack_ref,
    act_ref,
    slope_ref,
    t_low_ref,
    t_sum_ref,
    in_sem,
    out_sem,
):
    sources = (
        xt_hbm, tctx_hbm, two_hbm, xs_hbm, sctx_hbm, tin_hbm, tout_hbm, wo_hbm, w1_hbm, w2_hbm, wh_hbm
    )
    targets = (xt_ref, tctx_ref, two_ref, xs_ref, sctx_ref, tin_ref, tout_ref, wo_ref, w1_ref, w2_ref, wh_ref)
    loads = {
        name: pltpu.make_async_copy(source, target, in_sem.at[k])
        for k, (name, source, target) in enumerate(zip(DENSE_IN, sources, targets))
    }
    for c in loads.values():
        c.start()
    width_s, units_s = w1_ref.shape
    width_t, units_t = tin_ref.shape
    slots = xt_ref.shape[0]
    low = lambda v: v.astype(BF16)
    stores = []

    def store(source, target):
        stores.append(pltpu.make_async_copy(source, target, out_sem.at[len(stores)]))
        stores[-1].start()

    def columns(*refs):
        n = refs[0].shape[0]
        index = lax.broadcasted_iota(jnp.int32, (8, n), 0)
        block = jnp.zeros((8, n), F32)
        for k, ref in enumerate(refs):
            block = jnp.where(index == k, ref[...].reshape(1, n), block)
        turned = jnp.transpose(block)
        return [turned[:, k : k + 1] for k in range(len(refs))]

    t_gain_one, t_shift_one, t_gain_two, t_shift_two = columns(
        t_gain_one_ref, t_shift_one_ref, t_gain_two_ref, t_shift_two_ref
    )
    gain_one, shift_one, b_outer, gain_two, shift_two = columns(
        gain_one_ref, shift_one_ref, b_outer_ref, gain_two_ref, shift_two_ref
    )
    (b_inner,) = columns(b_inner_ref)
    spot = pad_heads()
    pack_ref[...] = jnp.zeros_like(pack_ref)
    act_ref[units_s:, :] = jnp.ones((act_ref.shape[0] - units_s, slots), BF16)
    for name in ("xt", "tctx", "two"):
        loads[name].wait()
    start = jnp.transpose(xt_ref[...]).astype(F32) + tn(two_ref[...], tctx_ref[...])
    t_normed = normalize(start, t_gain_one, t_shift_one)[0]
    t_low_ref[...] = low(t_normed)
    t_sum_ref[...] = t_normed
    for name in ("xs", "sctx", "tin", "tout"):
        loads[name].wait()

    def feed_forward(c, carry):
        units = pl.ds(pl.multiple_of(c * width_t, width_t), width_t)
        pre = tn(tin_ref[:, units], t_low_ref[...])
        active = low(0.5 * pre * (1.0 + lax.erf(pre * ROOT_HALF)))
        t_sum_ref[...] += tn(tout_ref[units, :], active)
        return carry

    lax.fori_loop(0, units_t // width_t, feed_forward, 0)
    target = normalize(t_sum_ref[...], t_gain_two, t_shift_two)[0]
    for name in ("wo", "w1", "w2", "wh"):
        loads[name].wait()
    wop = low(nn(spot, wo_ref[...]))
    context = sctx_ref[...]
    context_low = low(context)
    normed, unit_one, rscale_one = normalize(
        xs_ref[...].astype(F32) + tn(wop, context_low), gain_one, shift_one
    )
    normed_low = low(normed)
    pre = tn(w1_ref[...], normed_low) + b_inner
    half = 0.5 * (1.0 + lax.erf(pre * ROOT_HALF))
    slope_ref[...] = half + pre * (ROOT_PI * jnp.exp(-0.5 * pre * pre))
    act_ref[:units_s, :] = low(pre * half)
    student, unit_two, rscale_two = normalize(
        normed + nn(w2_ref[...], act_ref[:units_s, :]) + b_outer, gain_two, shift_two
    )
    student_low = low(student)
    out_ref[...] = student_low
    store(out_ref, out_hbm)
    gap = tn(wh_ref[...], student_low) - target
    filled = rows_ref[2:3, :]
    masked = filled * gap
    d_proj = low(2.0 * masked)
    third = slice(2 * BLOCK, 2 * BLOCK + width_s)
    pack_ref[third, :width_t] = low(nt(student_low, d_proj))
    d_student = nn(wh_ref[...], d_proj)
    d_two = normalize_back(d_student, unit_two, rscale_two, gain_two)
    d_outer = low(d_two)
    main = units_s // 128 * 128
    spare = units_s - main
    strip = 3 * BLOCK
    pack_ref[:width_s, :main] = low(nt(d_outer, act_ref[:main, :]))
    pack_ref[strip : strip + STRIP, STRIP_OUTER : STRIP_OUTER + width_s] = low(
        nt(act_ref[main : main + STRIP, :], d_outer)
    )
    store(pack_ref.at[:BLOCK], pack_hbm.at[:BLOCK])
    d_inner = low(tn(w2_ref[...], d_outer) * slope_ref[...])
    ones = jnp.ones((8, slots), BF16)
    pack_ref[BLOCK : BLOCK + width_s, :main] = low(nt(normed_low, d_inner[:main]))
    pack_ref[BLOCK + width_s : BLOCK + width_s + 8, :main] = low(nt(ones, d_inner[:main]))
    pack_ref[strip : strip + spare, :width_s] = low(nt(d_inner[main:], normed_low))
    pack_ref[strip : strip + spare, STRIP_BIAS : STRIP_BIAS + 8] = low(nt(d_inner[main:], ones))
    store(pack_ref.at[BLOCK : 2 * BLOCK], pack_hbm.at[BLOCK : 2 * BLOCK])
    d_normed = nn(w1_ref[...], d_inner) + d_two
    d_one = normalize_back(d_normed, unit_one, rscale_one, gain_one)
    dres_ref[...] = d_one
    store(dres_ref, dres_hbm)
    d_att = low(d_one)
    gwo = low(nt(context_low, d_att))
    pack_ref[third, width_t : width_t + width_s] = low(tn(spot, gwo))
    d_context = nn(wop, d_att)
    row = lax.broadcasted_iota(jnp.int32, (PAD, slots), 0)
    for head in range(HEADS):
        pair, h = head // 2, head % 2
        inverse = stats_ref[pair, h : h + 1, :]
        cross = stats_ref[pair, 2 + h : 3 + h, :]
        rows = slice(head * PAD, (head + 1) * PAD)
        part = low(d_context[rows] * inverse).astype(F32)
        delta = -jnp.sum(part * context[rows], axis=0, keepdims=True) - inverse * cross
        high = low(delta).astype(F32)
        rest = delta - high
        middle = low(rest).astype(F32)
        part = jnp.where(row == SLOT_ONE, high, part)
        part = jnp.where(row == SLOT_ONE + 1, middle, part)
        part = jnp.where(row == SLOT_ONE + 2, rest - middle, part)
        dctx_ref[rows, :] = low(part)
    store(dctx_ref, dctx_hbm)
    lane = lax.broadcasted_iota(jnp.int32, (width_s, 128), 1)
    sums = jnp.zeros((width_s, 128), F32)
    for k, values in enumerate((d_normed * unit_one, d_normed, d_student * unit_two, d_student)):
        sums = jnp.where(lane == k, jnp.sum(fold_lanes(values), axis=1, keepdims=True), sums)
    pack_ref[strip + spare : strip + spare + 8, :width_s] = low(jnp.transpose(sums)[:8])
    square = jnp.sum(fold_lanes(masked * gap).reshape(-1, 8, 128), axis=0)
    row = lax.broadcasted_iota(jnp.int32, (8, 128), 0)
    for c in range(slots // 128):
        square += jnp.where(row == c % 8, width_t * loss_ref[0:1, c * 128 : (c + 1) * 128], 0.0)
    pack_ref[2 * BLOCK + width_s : 2 * BLOCK + width_s + 8, :128] = low(square)
    store(pack_ref.at[2 * BLOCK :], pack_hbm.at[2 * BLOCK :])
    for c in stores:
        c.wait()


def dense(packed_rows, big, small):
    xt, tctx, two, xs, sctx, tin, tout, wo, w1, w2, wh = big
    slots, width_t = xt.shape
    width_s, units_s = w1.shape
    padded = HEADS * PAD
    inner_pad = -(-units_s // 128) * 128
    sds = jax.ShapeDtypeStruct
    outs = [
        sds((width_s, slots), BF16),
        sds((padded, slots), BF16),
        sds((width_s, slots), F32),
        sds((packed_rows, units_s // 128 * 128), BF16),
    ]
    anywhere = pl.BlockSpec(memory_space=pl.ANY)
    return pl.pallas_call(
        dense_kernel,
        out_shape=outs,
        in_specs=[anywhere] * len(big) + [VMEM] * len(small),
        out_specs=[anywhere] * len(outs),
        scratch_shapes=[pltpu.VMEM(a.shape, a.dtype) for a in big]
        + [pltpu.VMEM(a.shape, a.dtype) for a in outs]
        + [
            pltpu.VMEM((inner_pad, slots), BF16),
            pltpu.VMEM((units_s, slots), F32),
            pltpu.VMEM((width_t, slots), BF16),
            pltpu.VMEM((width_t, slots), F32),
            pltpu.SemaphoreType.DMA((len(big),)),
            pltpu.SemaphoreType.DMA((6,)),
        ],
        compiler_params=pltpu.CompilerParams(vmem_limit_bytes=BIG),
    )(*big, *small)


def group_sizes():
    seq = lax.axis_size("seq")
    core = 2 if seq % 2 == 0 else 1
    chain = 4 if seq // core % 4 == 0 else 1
    return {"core": core, "batch": lax.axis_size("batch"), "chain": chain, "outer": seq // core // chain}


class Group:
    def __init__(self, name):
        batch, seq = lax.axis_index("batch"), lax.axis_index("seq")
        sizes = group_sizes()
        self.size = sizes[name]
        if name == "batch":
            self.place = batch
            self.device = lambda j: (j, seq)
        else:
            stride = {"core": 1, "chain": sizes["core"], "outer": sizes["core"] * sizes["chain"]}[name]
            self.place = seq // stride % self.size
            self.device = lambda j: (batch, seq + (j - self.place) * stride)

    def other(self, k):
        return (self.place + k) % self.size


class Chain:
    def __init__(self, names, source, scratch, local=None):
        self.names, self.source, self.local = names, source, local
        self.groups = [Group(n) for n in names]
        count = len(names)
        self.outer = Group("outer")
        self.received, self.sums = scratch[:count], scratch[count : 2 * count]
        self.around, self.whole, self.send, self.arrive = scratch[2 * count :]
        rows = self.whole.shape[0]
        self.rows, self.base, base = [], [], 0
        for g in self.groups:
            self.base.append(base)
            rows //= g.size
            base = base + g.place * rows
            self.rows.append(rows)
        self.mine = base
        self.sem = 0
        self.pending = []

    @staticmethod
    def scratch(names, rows, lanes):
        received, sums, copies = [], [], 0
        total, sizes = rows, group_sizes()
        for size in (sizes[n] for n in names):
            rows = rows // size
            received.append(pltpu.VMEM((max(size - 1, 1), rows, lanes), BF16))
            sums.append(pltpu.VMEM((rows, lanes), BF16))
            copies += 2 * (size - 1)
        copies = max(copies + sizes["outer"] - 1, 1)
        return (
            received
            + sums
            + [
                pltpu.VMEM((max(sizes["outer"] - 1, 1), rows, lanes), BF16),
                pltpu.VMEM((total, lanes), BF16),
                pltpu.SemaphoreType.DMA((copies,)),
                pltpu.SemaphoreType.DMA((copies,)),
            ]
        )

    def copy(self, ends):
        at = self.sem
        self.sem += 1

        def form():
            source, target, device = ends()
            return pltpu.make_async_remote_copy(
                src_ref=source,
                dst_ref=target,
                send_sem=self.send.at[at],
                recv_sem=self.arrive.at[at],
                device_id=device,
                device_id_type=MESH,
            )

        form().start()
        self.pending.append(form)

    def scatter(self, k):
        g, rows = self.groups[k], self.rows[k]
        source = self.source if k == 0 else self.sums[k - 1]

        def ends(step):
            other = g.other(step)
            there = pl.ds(pl.multiple_of(other * rows, 16), rows)
            return source.at[there], self.received[k].at[step - 1], g.device(other)

        for step in range(1, g.size):
            self.copy(partial(ends, step))

    def wait(self):
        for form in self.pending:
            form().wait()
        self.pending = []

    def add(self, k):
        self.wait()
        g, rows = self.groups[k], self.rows[k]
        source = self.source if k == 0 else self.sums[k - 1]
        if k == 0 and self.local is not None:
            total = self.local[...].astype(F32)
        else:
            total = source[pl.ds(pl.multiple_of(g.place * rows, 16), rows), :].astype(F32)
        for step in range(1, g.size):
            total = total + self.received[k][step - 1].astype(F32)
        total = total.astype(BF16)
        if k < len(self.groups) - 1 or self.outer.size > 1:
            self.sums[k][...] = total
        if k == len(self.groups) - 1:
            if self.outer.size > 1:
                total = self.exchange(total)
            self.whole[pl.ds(pl.multiple_of(self.mine, 16), rows), :] = total

    def exchange(self, total):
        g = self.outer

        def ends(step):
            return self.sums[-1], self.around.at[step - 1], g.device(g.other(step))

        for step in range(1, g.size):
            self.copy(partial(ends, step))
        self.wait()
        total = total.astype(F32)
        for step in range(1, g.size):
            total = total + self.around[step - 1].astype(F32)
        return total.astype(BF16)

    def gather(self, k):
        g, rows = self.groups[k], self.rows[k]

        def ends(step):
            here = self.whole.at[pl.ds(pl.multiple_of(self.base[k] + g.place * rows, 16), rows)]
            return here, here, g.device(g.other(step))

        for step in range(1, g.size):
            self.copy(partial(ends, step))

    def advance(self, stage):
        count = len(self.groups)
        if 0 < stage <= count:
            self.add(stage - 1)
        else:
            self.wait()
        if stage < count:
            self.scatter(stage)
        elif stage < 2 * count:
            self.gather(2 * count - 1 - stage)


EARLY = (
    (0, 384, ("core", "batch", "chain")),
    (384, 768, ("core", "batch", "chain")),
    (768, 1152, ("core", "chain", "batch")),
)
LATE = (
    (0, 128, ("core", "batch", "chain")),
    (128, 256, ("core", "batch", "chain")),
    (256, 384, ("core", "chain", "batch")),
)


def back_kernel(
    windows,
    sq_hbm,
    skv_hbm,
    dctx_hbm,
    e_hbm,
    g_hbm,
    pack_hbm,
    xs_hbm,
    dres_hbm,
    wq_hbm,
    wk_hbm,
    wv_hbm,
    rows_ref,
    dx_ref,
    early_ref,
    late_ref,
    sq_ref,
    skv_ref,
    dctx_ref,
    e_ref,
    g_ref,
    half_ref,
    xs_ref,
    dres_ref,
    wq_ref,
    wk_ref,
    wv_ref,
    in_sem,
    block_sem,
    dq_ref,
    dkv_ref,
    give_ref,
    take_ref,
    qkv_ref,
    halo_send,
    halo_arrive,
    out_sem,
    *scratch,
):
    step = pl.program_id(0)
    w = (windows - step) % windows
    slots = windows * WIN
    width_s = xs_ref.shape[0]
    batch, seq = lax.axis_index("batch"), lax.axis_index("seq")
    peers = lax.axis_size("seq")
    chains, used = [], 0
    for source, local, cuts in ((pack_hbm, half_ref, EARLY), (qkv_ref, None, LATE)):
        for first, last, names in cuts:
            size = 2 * len(names) + 4
            mine = local.at[:, first:last] if local is not None else None
            chains.append(Chain(names, source.at[:, first:last], scratch[used : used + size], mine))
            used += size
    soon, late = chains[: len(EARLY)], chains[len(EARLY) :]
    first_seq, last_seq = seq == 0, seq == peers - 1

    def halo(side):
        return pltpu.make_async_remote_copy(
            src_ref=give_ref.at[side],
            dst_ref=take_ref.at[1 - side],
            send_sem=halo_send.at[side],
            recv_sem=halo_arrive.at[1 - side],
            device_id=(batch, seq - 1 + 2 * side),
            device_id_type=MESH,
        )

    half_rows = half_ref.shape[0]
    ends = {
        "half": (pack_hbm.at[pl.ds(pl.multiple_of(seq % group_sizes()["core"] * half_rows, 16), half_rows)], half_ref),
        "sq": (sq_hbm, sq_ref),
        "skv": (skv_hbm, skv_ref),
        "dctx": (dctx_hbm, dctx_ref),
        "xs": (xs_hbm, xs_ref),
        "dres": (dres_hbm, dres_ref),
        "wq": (wq_hbm, wq_ref),
        "wk": (wk_hbm, wk_ref),
        "wv": (wv_hbm, wv_ref),
    }
    load = lambda name: pltpu.make_async_copy(*ends[name], in_sem.at[list(ends).index(name)])

    def blocks(number):
        slot, window = number % 2, (windows - number) % windows
        return [
            pltpu.make_async_copy(source.at[window], target.at[slot], block_sem.at[k, slot])
            for k, (source, target) in enumerate(((e_hbm, e_ref), (g_hbm, g_ref)))
        ]

    @pl.when(step == 0)
    def _():
        load("half").start()
        dkv_ref[...] = jnp.zeros_like(dkv_ref)
        take_ref[...] = jnp.zeros_like(take_ref)
        qkv_ref[...] = jnp.zeros_like(qkv_ref)
        barrier = pltpu.get_barrier_semaphore()
        count = 0
        for g in (Group(n) for n in ("core", "batch", "chain", "outer")):
            for k in range(1, g.size):
                pl.semaphore_signal(barrier, inc=1, device_id=g.device(g.other(k)), device_id_type=MESH)
                count += 1

        for move in (1, peers - 1):
            pl.semaphore_signal(
                barrier, inc=1, device_id=(batch, (seq + move) % peers), device_id_type=MESH
            )
        pl.semaphore_wait(barrier, count + 2)

        for c in soon:
            c.advance(0)
        for c in blocks(0):
            c.start()
        for name in ("sq", "skv", "dctx"):
            load(name).start()
        for c in blocks(1):
            c.start()
        for name in ("xs", "dres", "wq", "wk", "wv"):
            load(name).start()
        for name in ("sq", "skv", "dctx", "half"):
            load(name).wait()

    for c in blocks(step):
        c.wait()
    slot = step % 2
    at = pl.multiple_of(w * WIN, WIN)
    left = pl.ds(at, WIN)
    own = pl.ds(pl.multiple_of(at + WIN, WIN), WIN)
    right = pl.ds(pl.multiple_of(at + 2 * WIN, WIN), WIN)
    early_row, late_row = rows_ref[0:1, left], rows_ref[1:2, left]
    early_low, late_low = early_row.astype(BF16), late_row.astype(BF16)

    def one_head(head):
        rows = pl.ds(pl.multiple_of(head * PAD, PAD), PAD)
        query, grad = sq_ref[rows, left], dctx_ref[rows, left]
        stacked = lambda a: jnp.concatenate([a * early_low, a * late_low], axis=0)
        query_fold, grad_fold = stacked(query), stacked(grad)
        beside = lambda k: jnp.concatenate([skv_ref[k, rows, left], skv_ref[k, rows, right]], axis=0)
        keys_fold, values_fold = beside(0), beside(1)
        keys, values = skv_ref[0, rows, own], skv_ref[1, rows, own]
        e_own, e_side = e_ref[slot, head, :WIN, :], e_ref[slot, head, WIN:, :]
        d_own = (e_own.astype(F32) * (tn(values, grad) + g_ref[slot, head, :WIN, :].astype(F32))).astype(BF16)
        d_side = (
            e_side.astype(F32) * (tn(values_fold, grad_fold) + g_ref[slot, head, WIN:, :].astype(F32))
        ).astype(BF16)
        side = nn(keys_fold, d_side)
        d_query = nn(keys, d_own) + early_row * side[:PAD] + late_row * side[PAD:]
        dq_ref[rows, left] = (d_query * HD_S**-0.5).astype(BF16)
        for k, (a, a_fold, b, b_fold, scale) in enumerate(
            ((query, query_fold, d_own, d_side, 1.0 / LOG2E), (grad, grad_fold, e_own, e_side, None))
        ):
            fix = (lambda v: v * scale) if scale else (lambda v: v)
            side = fix(nt(a_fold, b_fold))
            dkv_ref[k, rows, own] += fix(nt(a, b))
            dkv_ref[k, rows, left] += side[:PAD]
            dkv_ref[k, rows, right] += side[PAD:]

    def body(pair, carry):
        one_head(2 * pair)
        one_head(2 * pair + 1)
        return carry

    def send_halo():
        for side, lanes in ((0, slice(0, WIN)), (1, slice(WIN + slots, 2 * WIN + slots))):
            give_ref[side] = dkv_ref[:, :, lanes].astype(BF16)

        @pl.when(jnp.logical_not(first_seq))
        def _():
            halo(0).start()

        @pl.when(jnp.logical_not(last_seq))
        def _():
            halo(1).start()

    def advance(which, stage):
        for c in which:
            c.advance(stage)

    half = PAIRS // 2
    plan = {
        (0, 0): [partial(advance, soon, 1)],
        (1, 1): [send_halo],
        (2, 0): [partial(advance, soon, 2)],
        (3, 0): [partial(advance, soon, 3)],
    }
    for part in range(2):
        lax.fori_loop(part * half, (part + 1) * half, body, 0)
        for k in range(windows):
            for action in plan.get((k, part), []):
                pl.when(step == k)(action)

    @pl.when(step < windows - 2)
    def _():
        for c in blocks(step + 2):
            c.start()

    @pl.when(step == windows - 1)
    def _():
        for name in ("xs", "dres", "wq", "wk", "wv"):
            load(name).wait()

        @pl.when(jnp.logical_not(first_seq))
        def _():
            halo(0).wait_send()
            halo(1).wait_recv()

        @pl.when(jnp.logical_not(last_seq))
        def _():
            halo(1).wait_send()
            halo(0).wait_recv()

        spot = pad_heads()
        plains = []
        for k in range(3):
            if k == 0:
                grad = dq_ref[...]
            else:
                mine = dkv_ref[k - 1, :, WIN : WIN + slots]
                first = mine[:, :WIN] + take_ref[0, k - 1].astype(F32)
                last = mine[:, slots - WIN :] + take_ref[1, k - 1].astype(F32)
                grad = jnp.concatenate([first, mine[:, WIN : slots - WIN], last], axis=1).astype(BF16)
            plain = tn(spot, grad).astype(BF16)
            plains.append(plain)
            qkv_ref[k * BLOCK : k * BLOCK + width_s, :width_s] = nt(xs_ref[...], plain).astype(BF16)
        advance(soon, 4)
        advance(late, 0)
        total = dres_ref[...]
        for w_ref, plain in zip((wq_ref, wk_ref, wv_ref), plains):
            total = total + nn(w_ref[...], plain)
        dx_ref[...] = total.astype(BF16)
        advance(late, 1)
        advance(late, 2)
        advance(soon, 5)
        advance(late, 3)
        advance(soon, 6)

        def put(group, cuts, target, first_sem):
            made = []
            for n, (c, (first, last, _)) in enumerate(zip(group, cuts)):
                made.append(pltpu.make_async_copy(c.whole, target.at[:, first:last], out_sem.at[first_sem + n]))
                made[-1].start()
            return made

        copies = put(soon, EARLY, early_ref, 0)
        advance(late, 4)
        advance(late, 5)
        advance(late, 6)
        copies += put(late, LATE, late_ref, len(EARLY))
        for c in copies:
            c.wait()


def back(sq, skv, dctx, e, g, rows, pack, xs, dres, wq, wk, wv):
    padded, slots = sq.shape
    windows = slots // WIN
    width_s = xs.shape[0]
    packed_rows = pack.shape[0]
    anywhere = pl.BlockSpec(memory_space=pl.ANY)
    held = lambda a: pltpu.VMEM(a.shape, a.dtype)
    scratch = [held(sq), held(skv), held(dctx)]
    scratch += [pltpu.VMEM((2,) + a.shape[1:], a.dtype) for a in (e, g)]
    scratch += [pltpu.VMEM((packed_rows // group_sizes()["core"], pack.shape[1]), BF16)]
    scratch += [held(a) for a in (xs, dres, wq, wk, wv)]
    scratch += [
        pltpu.SemaphoreType.DMA((9,)),
        pltpu.SemaphoreType.DMA((2, 2)),
        pltpu.VMEM((padded, slots), BF16),
        pltpu.VMEM((2, padded, slots + 2 * WIN), F32),
        pltpu.VMEM((2, 2, padded, WIN), BF16),
        pltpu.VMEM((2, 2, padded, WIN), BF16),
        pltpu.VMEM((packed_rows, QKV_LANES), BF16),
        pltpu.SemaphoreType.DMA((2,)),
        pltpu.SemaphoreType.DMA((2,)),
        pltpu.SemaphoreType.DMA((len(EARLY) + len(LATE),)),
    ]
    for first, last, names in EARLY + LATE:
        scratch += Chain.scratch(names, packed_rows, last - first)
    return pl.pallas_call(
        partial(back_kernel, windows),
        grid=(windows,),
        out_shape=[
            jax.ShapeDtypeStruct((width_s, slots), BF16),
            jax.ShapeDtypeStruct(pack.shape, BF16),
            jax.ShapeDtypeStruct((packed_rows, QKV_LANES), BF16),
        ],
        in_specs=[anywhere] * 11 + [VMEM],
        out_specs=[pl.BlockSpec((width_s, slots), lambda i: (0, 0)), anywhere, anywhere],
        scratch_shapes=scratch,
        compiler_params=pltpu.CompilerParams(
            vmem_limit_bytes=BIG,
            dimension_semantics=("arbitrary",),
            collective_id=0,
            has_side_effects=True,
        ),
    )(sq, skv, dctx, e, g, pack, xs, dres, wq, wk, wv, rows)


def unpack_kernel(
    every,
    width_t,
    early_hbm,
    late_hbm,
    dx_in_ref,
    dx_ref,
    loss_ref,
    gq_hbm,
    gk_hbm,
    gv_hbm,
    gwo_hbm,
    ginner_hbm,
    gouter_hbm,
    ghid_hbm,
    bouter_ref,
    binner_ref,
    gain_one_ref,
    shift_one_ref,
    gain_two_ref,
    shift_two_ref,
    early_ref,
    late_ref,
    gq_ref,
    gk_ref,
    gv_ref,
    gwo_ref,
    ginner_ref,
    gouter_ref,
    ghid_ref,
    in_sem,
    out_sem,
):
    width_s = gq_ref.shape[0]
    units = ginner_ref.shape[1]
    scale = 1.0 / every
    full = lambda v: v.astype(F32) * scale
    main = units // 128 * 128
    rest = units - main
    cuts = (slice(3 * BLOCK, 3 * BLOCK + STRIP),) + tuple(slice(k * BLOCK, (k + 1) * BLOCK) for k in range(3))
    loads = [pltpu.make_async_copy(early_hbm.at[c], early_ref.at[c], in_sem.at[k]) for k, c in enumerate(cuts)]
    loads.append(pltpu.make_async_copy(late_hbm, late_ref, in_sem.at[4]))
    for c in loads:
        c.start()
    stores = []

    def store(source, target):
        stores.append(pltpu.make_async_copy(source, target, out_sem.at[len(stores)]))
        stores[-1].start()

    dx_ref[...] = dx_in_ref[...]
    loads[0].wait()
    strip = full(early_ref[3 * BLOCK : 3 * BLOCK + STRIP, :])
    turned = lambda at, n: jnp.transpose(strip[:, at : at + n])
    for k, ref in enumerate((gain_one_ref, shift_one_ref, gain_two_ref, shift_two_ref)):
        ref[...] = strip[rest + k, :width_s]
    bouter_ref[...] = strip[rest, STRIP_OUTER : STRIP_OUTER + width_s]
    loads[1].wait()
    gouter_ref[:, :main] = full(early_ref[:width_s, :main])
    gouter_ref[:, main:] = turned(STRIP_OUTER, STRIP_BIAS - STRIP_OUTER)[:width_s, :rest]
    store(gouter_ref, gouter_hbm)
    loads[2].wait()
    ginner_ref[:, :main] = full(early_ref[BLOCK : BLOCK + width_s, :main])
    ginner_ref[:, main:] = turned(0, STRIP_OUTER)[:width_s, :rest]
    store(ginner_ref, ginner_hbm)
    first = full(early_ref[BLOCK + width_s : BLOCK + width_s + 8, :main])[0:1]
    binner_ref[...] = jnp.concatenate([first, turned(STRIP_BIAS, 128)[0:1, :rest]], axis=1)[0]
    loads[3].wait()
    third = slice(2 * BLOCK, 2 * BLOCK + width_s)
    ghid_ref[...] = full(early_ref[third, :width_t])
    store(ghid_ref, ghid_hbm)
    gwo_ref[...] = full(early_ref[third, width_t : width_t + width_s])
    store(gwo_ref, gwo_hbm)
    loads[4].wait()
    for k, (ref, hbm) in enumerate(((gq_ref, gq_hbm), (gk_ref, gk_hbm), (gv_ref, gv_hbm))):
        ref[...] = full(late_ref[k * BLOCK : k * BLOCK + width_s, :width_s])
        store(ref, hbm)
    part = early_ref[2 * BLOCK + width_s : 2 * BLOCK + width_s + 8, :128].astype(F32)
    total = jnp.sum(jnp.sum(part, axis=0, keepdims=True), axis=1, keepdims=True)
    loss_ref[...] = total
    for c in stores:
        c.wait()


def unpack(every, width_t, units, early, late, dx):
    width_s = dx.shape[0]
    sds = lambda *shape: jax.ShapeDtypeStruct(shape, F32)
    square = sds(width_s, width_s)
    large = [square, square, square, square, sds(width_s, units), sds(width_s, units), sds(width_s, width_t)]
    vectors = [sds(width_s), sds(units)] + [sds(width_s)] * 4
    anywhere = pl.BlockSpec(memory_space=pl.ANY)
    return pl.pallas_call(
        partial(unpack_kernel, every, width_t),
        out_shape=[jax.ShapeDtypeStruct(dx.shape, BF16), sds(1, 1)] + large + vectors,
        in_specs=[anywhere, anywhere, VMEM],
        out_specs=[VMEM] * 2 + [anywhere] * len(large) + [VMEM] * len(vectors),
        scratch_shapes=[pltpu.VMEM(early.shape, BF16), pltpu.VMEM(late.shape, BF16)]
        + [pltpu.VMEM(a.shape, F32) for a in large]
        + [pltpu.SemaphoreType.DMA((5,)), pltpu.SemaphoreType.DMA((len(large),))],
        compiler_params=pltpu.CompilerParams(vmem_limit_bytes=BIG),
    )(early, late, dx)


def local(
    inputs,
    teacher_input,
    filled_slot_mask,
    seg_lengths,
    query_weight,
    key_weight,
    value_weight,
    w_output,
    gain_one,
    shift_one,
    w_inner,
    b_inner,
    w_outer,
    b_outer,
    gain_two,
    shift_two,
    w_hidden,
    teacher_query_weight,
    teacher_key_weight,
    teacher_value_weight,
    teacher_output,
    teacher_gain_one,
    teacher_shift_one,
    teacher_inner,
    teacher_outer,
    teacher_gain_two,
    teacher_shift_two,
):
    xs = jnp.transpose(inputs[0])
    xt = teacher_input[0]
    slots, width_t = xt.shape
    width_s = xs.shape[0]
    stats, loss_rows, rows, tctx, sctx, sq, skv, e, g = attend(
        filled_slot_mask,
        seg_lengths,
        xt,
        xs,
        teacher_query_weight,
        teacher_key_weight,
        teacher_value_weight,
        query_weight,
        key_weight,
        value_weight,
    )
    devices = lax.axis_size("seq") * lax.axis_size("batch")
    sizes = group_sizes()
    unit = 16 * sizes["core"] * sizes["batch"] * sizes["chain"]
    packed_rows = -(-3 * BLOCK // unit) * unit
    out, dctx, dres, pack = dense(
        packed_rows,
        (
            xt,
            tctx,
            teacher_output,
            xs,
            sctx,
            teacher_inner,
            teacher_outer,
            w_output,
            w_inner,
            jnp.transpose(w_outer),
            w_hidden,
        ),
        (stats, rows, loss_rows)
        + (
            teacher_gain_one,
            teacher_shift_one,
            teacher_gain_two,
            teacher_shift_two,
            gain_one,
            shift_one,
            b_outer,
            gain_two,
            shift_two,
            b_inner,
        ),
    )
    dx, early, late = back(sq, skv, dctx, e, g, rows, pack, xs, dres, query_weight, key_weight, value_weight)
    dx, loss, gq, gk, gv, gwo, ginner, gouter, ghid, *vectors = unpack(
        slots * devices, width_t, w_inner.shape[1], early, late, dx
    )
    g_b_outer, g_b_inner, g_gain_one, g_shift_one, g_gain_two, g_shift_two = vectors
    return (
        jnp.transpose(out)[None],
        jnp.transpose(dx)[None],
        loss[0, 0] / (slots * devices * width_t),
        gq,
        gk,
        gv,
        gwo,
        g_gain_one,
        g_shift_one,
        ginner,
        g_b_inner,
        jnp.transpose(gouter),
        g_b_outer,
        g_gain_two,
        g_shift_two,
        ghid,
    )


def solution(mesh):
    row_split = P("batch", "seq", None)
    return jax.shard_map(
        local,
        mesh=mesh,
        in_specs=(row_split, row_split, P("batch", None), P("batch", None)) + (P(),) * 23,
        out_specs=(row_split, row_split) + (P(),) * 14,
        check_vma=False,
    )
```

profile of v0, /device:TPU:0, one launch (start us, length us, event | category | flops | bytes accessed | tf_op | source)
XLA Modules:
  0.0 148.2 jit_solution(6021675941307770480)
XLA Ops:
  0.6 43.3 %shard_map.378 = (f32[6,8,1024]{2,1,0:T(8,128)}, f32[8,1024]{1,0:T(8,128)}, f32[8,1024]{1,0:T(8,128)}, bf16[768,1024]{1,0:T(8,128)(2,1)}, f32[384,1024]{1,0:T(8,...) custom-call(s32[1,8192]{1,0:T(1,128)} %mask_ref.1, ...), custom_call_target="tpu_custom_call" | custom-call | tf_op jit(solution)/shard_map/pallas_call | solution.py:432
  43.9 32.9 %shard_map.379 = (bf16[312,1024]{1,0:T(8,128)(2,1)}, bf16[384,1024]{1,0:T(8,128)(2,1)}, f32[312,1024]{1,0:T(8,128)}, bf16[1024,1152]{1,0:T(8,128)(2,1)}) custom-call(bf16[1024,768]{1,0:T(8,128)(2,1)} %bitcast.14, bf16[768,1024]{1,0:T(8,128)(2,1)} %get-tuple-element.47.tctx_hbm, bf16[768,768]{1,0:T(8,128)(2,1)} %two_hbm.1, bf16[312,1024]{1,0:T(8,128)(2,1)} %bitcast.16, ...), custom_call_target="tpu_custom_call" | custom-call | tf_op jit(solution)/shard_map/pallas_call | solution.py:710
  76.8 63.6 %shard_map.380 = (bf16[312,1024]{1,0:T(8,128)(2,1)}, bf16[1024,1152]{1,0:T(8,128)(2,1)}, bf16[1024,384]{1,0:T(8,128)(2,1)}) custom-call(bf16[384,1024]{1,0:T(8,128)(2,1)} %get-tuple-element.53.sq_hbm, bf16[2,384,1536]{2,1,0:T(8,128)(2,1)} %get-tuple-element.54.skv_hbm, bf16[384,1024]{1,0:T(8,128)(2,1)} %get-tuple-element.55.dctx_hbm, ...), custom_call_target="tpu_custom_call" | custom-call | tf_op jit(solution)/shard_map/pallas_call | solution.py:1168
  140.4 6.1 %shard_map.381 = (bf16[312,1024]{1,0:T(8,128)(2,1)}, f32[1,1]{1,0:T(1,128)}, f32[312,312]{1,0:T(8,128)}, f32[312,312]{1,0:T(8,128)}, f32[312,312]{1,0:T(8,128)},...) custom-call(bf16[1024,1152]{1,0:T(8,128)(2,1)} %get-tuple-element.60, ...), custom_call_target="tpu_custom_call" | custom-call | tf_op jit(solution)/shard_map/pallas_call | solution.py:1279
where the time goes:
time: 149 us; the launch traced here: 148 us
  Pallas kernels  146 us (98%)
  between operations  2.45 us (2%)
    pallas_call x1, Pallas kernels, back(): pl.pallas_call(partial(back_kernel, windows), grid=(windows,), out_shape=...  63.6 us
    pallas_call x1, Pallas kernels, attend(): pl.pallas_call(partial(attend_kernel, windows, row_windows), out_shape=(s...  43.3 us
    pallas_call x1, Pallas kernels, dense(): pl.pallas_call(dense_kernel, out_shape=outs, in_specs=[anywhere] * len(bi...  32.9 us
    pallas_call x1, Pallas kernels, unpack(): pl.pallas_call(partial(unpack_kernel, every, width_t), out_shape=[jax.Sha...  6.05 us

commit v1 on v0

--- a/solution.py
+++ b/solution.py
@@ -1099,6 +1099,7 @@
             halo(1).wait_send()
             halo(0).wait_recv()
 
+        advance(soon, 4)
         spot = pad_heads()
         plains = []
         for k in range(3):
@@ -1112,7 +1113,6 @@
             plain = tn(spot, grad).astype(BF16)
             plains.append(plain)
             qkv_ref[k * BLOCK : k * BLOCK + width_s, :width_s] = nt(xs_ref[...], plain).astype(BF16)
-        advance(soon, 4)
         advance(late, 0)
         total = dres_ref[...]
         for w_ref, plain in zip((wq_ref, wk_ref, wv_ref), plains):

time: 149 us -> 147 us (0.987)
  Pallas kernels: 146 us -> 144 us
    pallas_call x1, Pallas kernels: 63.6 us -> 62.1 us  [back(): pl.pallas_call(partial(back_kernel, windows), grid=(windows,), out_shape=...]
where the time goes in v1:
time: 147 us
  Pallas kernels  144 us (98%)
  between operations  2.45 us (2%)
    pallas_call x1, Pallas kernels, back(): pl.pallas_call(partial(back_kernel, windows), grid=(windows,), out_shape=...  62.1 us
    pallas_call x1, Pallas kernels, attend(): pl.pallas_call(partial(attend_kernel, windows, row_windows), out_shape=(s...  43.3 us
    pallas_call x1, Pallas kernels, dense(): pl.pallas_call(dense_kernel, out_shape=outs, in_specs=[anywhere] * len(bi...  32.9 us
    pallas_call x1, Pallas kernels, unpack(): pl.pallas_call(partial(unpack_kernel, every, width_t), out_shape=[jax.Sha...  6.05 us

profile of v1, /device:TPU:0, one launch (start us, length us, event | category | flops | bytes accessed | tf_op | source)
XLA Modules:
  0.0 146.7 jit_solution(5975622031837304840)
XLA Ops:
  0.6 43.3 %shard_map.378 = (f32[6,8,1024]{2,1,0:T(8,128)}, f32[8,1024]{1,0:T(8,128)}, f32[8,1024]{1,0:T(8,128)}, bf16[768,1024]{1,0:T(8,128)(2,1)}, f32[384,1024]{1,0:T(8,...) custom-call(s32[1,8192]{1,0:T(1,128)} %mask_ref.1, ...), custom_call_target="tpu_custom_call" | custom-call | tf_op jit(solution)/shard_map/pallas_call | solution.py:432
  43.9 32.9 %shard_map.379 = (bf16[312,1024]{1,0:T(8,128)(2,1)}, bf16[384,1024]{1,0:T(8,128)(2,1)}, f32[312,1024]{1,0:T(8,128)}, bf16[1024,1152]{1,0:T(8,128)(2,1)}) custom-call(bf16[1024,768]{1,0:T(8,128)(2,1)} %bitcast.14, bf16[768,1024]{1,0:T(8,128)(2,1)} %get-tuple-element.47.tctx_hbm, bf16[768,768]{1,0:T(8,128)(2,1)} %two_hbm.1, bf16[312,1024]{1,0:T(8,128)(2,1)} %bitcast.16, ...), custom_call_target="tpu_custom_call" | custom-call | tf_op jit(solution)/shard_map/pallas_call | solution.py:710
  76.8 62.1 %shard_map.380 = (bf16[312,1024]{1,0:T(8,128)(2,1)}, bf16[1024,1152]{1,0:T(8,128)(2,1)}, bf16[1024,384]{1,0:T(8,128)(2,1)}) custom-call(bf16[384,1024]{1,0:T(8,128)(2,1)} %get-tuple-element.53.sq_hbm, bf16[2,384,1536]{2,1,0:T(8,128)(2,1)} %get-tuple-element.54.skv_hbm, bf16[384,1024]{1,0:T(8,128)(2,1)} %get-tuple-element.55.dctx_hbm, ...), custom_call_target="tpu_custom_call" | custom-call | tf_op jit(solution)/shard_map/pallas_call | solution.py:1168
  138.9 6.1 %shard_map.381 = (bf16[312,1024]{1,0:T(8,128)(2,1)}, f32[1,1]{1,0:T(1,128)}, f32[312,312]{1,0:T(8,128)}, f32[312,312]{1,0:T(8,128)}, f32[312,312]{1,0:T(8,128)},...) custom-call(bf16[1024,1152]{1,0:T(8,128)(2,1)} %get-tuple-element.60, ...), custom_call_target="tpu_custom_call" | custom-call | tf_op jit(solution)/shard_map/pallas_call | solution.py:1279

commit v2 on v1

--- a/solution.py
+++ b/solution.py
@@ -1190,8 +1190,8 @@
     width_t,
     early_hbm,
     late_hbm,
-    dx_in_ref,
-    dx_ref,
+    dx_in_hbm,
+    dx_hbm,
     loss_ref,
     gq_hbm,
     gk_hbm,
@@ -1235,7 +1235,7 @@
         stores.append(pltpu.make_async_copy(source, target, out_sem.at[len(stores)]))
         stores[-1].start()
 
-    dx_ref[...] = dx_in_ref[...]
+    store(dx_in_hbm, dx_hbm)
     loads[0].wait()
     strip = full(early_ref[3 * BLOCK : 3 * BLOCK + STRIP, :])
     turned = lambda at, n: jnp.transpose(strip[:, at : at + n])
@@ -1279,11 +1279,11 @@
     return pl.pallas_call(
         partial(unpack_kernel, every, width_t),
         out_shape=[jax.ShapeDtypeStruct(dx.shape, BF16), sds(1, 1)] + large + vectors,
-        in_specs=[anywhere, anywhere, VMEM],
-        out_specs=[VMEM] * 2 + [anywhere] * len(large) + [VMEM] * len(vectors),
+        in_specs=[anywhere] * 3,
+        out_specs=[anywhere, VMEM] + [anywhere] * len(large) + [VMEM] * len(vectors),
         scratch_shapes=[pltpu.VMEM(early.shape, BF16), pltpu.VMEM(late.shape, BF16)]
         + [pltpu.VMEM(a.shape, F32) for a in large]
-        + [pltpu.SemaphoreType.DMA((5,)), pltpu.SemaphoreType.DMA((len(large),))],
+        + [pltpu.SemaphoreType.DMA((5,)), pltpu.SemaphoreType.DMA((len(large) + 1,))],
         compiler_params=pltpu.CompilerParams(vmem_limit_bytes=BIG),
     )(early, late, dx)
 

time: 147 us -> 162 us (1.10)
  Pallas kernels: 144 us -> 159 us
    pallas_call x1, Pallas kernels: 6.05 us -> 21.2 us  [unpack(): pl.pallas_call(partial(unpack_kernel, every, width_t), out_shape=[jax.Sha...]
where the time goes in v2:
time: 162 us
  Pallas kernels  159 us (98%)
  between operations  2.45 us (2%)
    pallas_call x1, Pallas kernels, back(): pl.pallas_call(partial(back_kernel, windows), grid=(windows,), out_shape=...  62.1 us
    pallas_call x1, Pallas kernels, attend(): pl.pallas_call(partial(attend_kernel, windows, row_windows), out_shape=(s...  43.3 us
    pallas_call x1, Pallas kernels, dense(): pl.pallas_call(dense_kernel, out_shape=outs, in_specs=[anywhere] * len(bi...  32.9 us
    pallas_call x1, Pallas kernels, unpack(): pl.pallas_call(partial(unpack_kernel, every, width_t), out_shape=[jax.Sha...  21.2 us

profile of v2, /device:TPU:0, one launch (start us, length us, event | category | flops | bytes accessed | tf_op | source)
XLA Modules:
  0.0 161.9 jit_solution(5163383595191247423)
XLA Ops:
  0.6 43.3 %shard_map.378 = (f32[6,8,1024]{2,1,0:T(8,128)}, f32[8,1024]{1,0:T(8,128)}, f32[8,1024]{1,0:T(8,128)}, bf16[768,1024]{1,0:T(8,128)(2,1)}, f32[384,1024]{1,0:T(8,...) custom-call(s32[1,8192]{1,0:T(1,128)} %mask_ref.1, ...), custom_call_target="tpu_custom_call" | custom-call | tf_op jit(solution)/shard_map/pallas_call | solution.py:432
  43.9 32.9 %shard_map.379 = (bf16[312,1024]{1,0:T(8,128)(2,1)}, bf16[384,1024]{1,0:T(8,128)(2,1)}, f32[312,1024]{1,0:T(8,128)}, bf16[1024,1152]{1,0:T(8,128)(2,1)}) custom-call(bf16[1024,768]{1,0:T(8,128)(2,1)} %bitcast.14, bf16[768,1024]{1,0:T(8,128)(2,1)} %get-tuple-element.47.tctx_hbm, bf16[768,768]{1,0:T(8,128)(2,1)} %two_hbm.1, bf16[312,1024]{1,0:T(8,128)(2,1)} %bitcast.16, ...), custom_call_target="tpu_custom_call" | custom-call | tf_op jit(solution)/shard_map/pallas_call | solution.py:710
  76.8 62.1 %shard_map.380 = (bf16[312,1024]{1,0:T(8,128)(2,1)}, bf16[1024,1152]{1,0:T(8,128)(2,1)}, bf16[1024,384]{1,0:T(8,128)(2,1)}) custom-call(bf16[384,1024]{1,0:T(8,128)(2,1)} %get-tuple-element.53.sq_hbm, bf16[2,384,1536]{2,1,0:T(8,128)(2,1)} %get-tuple-element.54.skv_hbm, bf16[384,1024]{1,0:T(8,128)(2,1)} %get-tuple-element.55.dctx_hbm, ...), custom_call_target="tpu_custom_call" | custom-call | tf_op jit(solution)/shard_map/pallas_call | solution.py:1168
  138.9 21.2 %shard_map.381 = (bf16[312,1024]{1,0:T(8,128)(2,1)}, f32[1,1]{1,0:T(1,128)}, f32[312,312]{1,0:T(8,128)}, f32[312,312]{1,0:T(8,128)}, f32[312,312]{1,0:T(8,128)},...) custom-call(bf16[1024,1152]{1,0:T(8,128)(2,1)} %get-tuple-element.60, ...), custom_call_target="tpu_custom_call" | custom-call | tf_op jit(solution)/shard_map/pallas_call | solution.py:1279
